TPU v7x, 32 devices: a whole 2x2x4 slice. The times are simulated.
32 devices in a mesh: depth: 8 (over z, y), filt: 4 (over x, core).
Axes of the slice: x: 2, y: 2, z: 4, core: 2. Of those that a mesh axis runs over, the one named last changes fastest.
Arguments:
- features: bfloat16 [16, 128, 4096], P('depth', 'filt'), may hold values from -6 to 6
- first_kernel: bfloat16 [3, 3, 3, 256, 128], P(None, None, None, 'filt'), may hold values from -0.109375 to 0.109375
- first_bias: float32 [256], P('filt'), may hold values from -1.5 to 1.5
- second_kernel: bfloat16 [3, 3, 3, 256, 256], P(None, None, None, 'filt'), may hold values from -0.078125 to 0.078125
- second_bias: float32 [256], P('filt'), may hold values from -1.5 to 1.5
Outputs:
- activated: bfloat16 [16, 256, 4096], P('depth', 'filt')
All inputs are finite; a program needn't handle non-finite values.
Results may differ from a plain program's by a relative error of at most 0.0047.
Values may be sent and summed in bfloat16 or wider, within the bound.
A program may use at most 64 MiB of HBM per device.

v0:
```python
import jax
import jax.numpy as jnp
from jax import lax
from jax.sharding import PartitionSpec as P

SIDE = 64
REACH = 2


leak_slope = 0.3


def depth_padded(block, width):
    count = lax.axis_size("depth")
    forward = [(i, i + 1) for i in range(count - 1)]
    backward = [(target, source) for source, target in forward]
    low = lax.ppermute(block[block.shape[0] - width :], "depth", forward)
    high = lax.ppermute(block[:width], "depth", backward)
    return jnp.concatenate([low, block, high], axis=0)


def row_blocks(features, parts, rows):
    framed = jnp.pad(features, ((0, 0), (0, 0), (REACH * SIDE, REACH * SIDE)))
    span = (rows + 2 * REACH) * SIDE
    return jnp.stack(
        [framed[:, :, part * rows * SIDE : part * rows * SIDE + span] for part in range(parts)]
    )


def convolve(volume, kernel):
    return lax.conv_general_dilated(
        volume[None],
        kernel,
        (1, 1, 1),
        ((0, 0), (0, 0), (1, 1)),
        dimension_numbers=("NDHWC", "DHWOI", "NDHWC"),
        preferred_element_type=jnp.float32,
    )[0]


def activate(summed, bias):
    shifted = summed + bias
    return jnp.where(shifted > 0, shifted, leak_slope * shifted)


def inside(count, offset, limit):
    place = jnp.arange(count, dtype=jnp.int32) + offset
    return (place >= 0) & (place < limit)


def local(features, first_kernel, first_bias, second_kernel, second_bias):
    parts = lax.axis_size("filt")
    rows = SIDE // parts
    planes, share = features.shape[0], features.shape[1]
    channels = share * parts
    depth_limit = planes * lax.axis_size("depth")
    first_whole = lax.all_gather(first_kernel, "filt", axis=3, tiled=True)
    second_whole = lax.all_gather(second_kernel, "filt", axis=3, tiled=True)
    first_shift = lax.all_gather(first_bias, "filt", axis=0, tiled=True)
    second_shift = lax.all_gather(second_bias, "filt", axis=0, tiled=True)
    blocks = lax.all_to_all(row_blocks(features, parts, rows), "filt", 0, 0)
    mine = jnp.transpose(blocks, (1, 3, 0, 2)).reshape(planes, -1, channels)
    volume = depth_padded(mine, REACH).reshape(planes + 2 * REACH, rows + 2 * REACH, SIDE, channels)
    first_sum = convolve(volume, first_whole)
    hidden = activate(first_sum, first_shift)
    deep = inside(planes + 2, lax.axis_index("depth") * planes - 1, depth_limit)
    high = inside(rows + 2, lax.axis_index("filt") * rows - 1, SIDE)
    usable = deep[:, None] & high[None, :]
    hidden = jnp.where(usable[:, :, None, None], hidden, 0.0).astype(jnp.bfloat16)
    activated = activate(convolve(hidden, second_whole), second_shift).astype(jnp.bfloat16)
    flat = jnp.transpose(activated.reshape(planes, rows * SIDE, -1), (0, 2, 1))
    return lax.all_to_all(flat, "filt", 1, 2, tiled=True)


def solution(mesh):
    in_specs = (
        P("depth", "filt", None),
        P(None, None, None, "filt", None),
        P("filt"),
        P(None, None, None, "filt", None),
        P("filt"),
    )
    out_specs = P("depth", "filt", None)
    return jax.shard_map(local, mesh=mesh, in_specs=in_specs, out_specs=out_specs, check_vma=False)
```

profile of v0, /device:TPU:0, one launch (start us, length us, event | category | flops | bytes accessed | tf_op | source)
XLA Modules:
  0.0 117.2 jit_solution(6162203553146862826)
XLA Ops:
  6.5 0.7 all-gather.3.cloned.1.call-update
  7.3 0.7 all-gather.5.cloned.1.call-update
  8.0 1.2 %fusion.31 = (bf16[1,2,32,1280]{3,2,1,0:T(8,128)(2,1)S(1)}, bf16[1,2,32,1280]{3,2,1,0:T(8,128)(2,1)S(1)}, bf16[1,2,32,1280]{3,2,1,0:T(8,128)(2,1)S(1)}, bf16[1,2,32,1280]{3,2,1,0:T(8,128)(2,1)S(1)}) fusion(bf16[2,32,4096]{2,1,0:T(8,128)(2,1)} %param.5), kind=kLoop, calls=%fused_computation.34 | loop fusion | bytes 1507328 | tf_op jit(solution)/shard_map/stack | solution.py:25
  9.3 16.8 %all_to_all.23 = bf16[4,2,32,1280]{3,2,1,0:T(8,128)(2,1)S(1)} all-to-all(bf16[4,2,32,1280]{3,2,1,0:T(8,128)(2,1)S(1)} %pad_maximum_fusion), channel_id=1, replica_groups=mesh['depth'=8,'filt'=4] {'filt'}, dimensions={0} | all-to-all | bytes 1310720 | tf_op jit(solution)/shard_map/all_to_all | solution.py:61
  26.2 4.3 %collective-permute-start = (bf16[2,1280,128]{1,2,0:T(8,128)(2,1)S(1)}, bf16[2,1280,128]{1,2,0:T(8,128)(2,1)}, u32[]{:S(2)}, u32[]{:S(2)}) collective-permute-start(bf16[2,1280,128]{1,2,0:T(8,128)(2,1)S(1)} %bitcast.50), channel_id=1, source_target_pairs={{0,4},{4,8},{8,12},{12,16},{16,20},{20,24},{24,28},{1,5},{5,9},{9,... | collective-permute-start | bytes 1966088 | tf_op jit(solution)/shard_map/ppermute | solution.py:17
  30.5 1.3 %collective-permute-start.1 = (bf16[2,1280,128]{1,2,0:T(8,128)(2,1)S(1)}, bf16[2,1280,128]{1,2,0:T(8,128)(2,1)S(1)}, u32[]{:S(2)}, u32[]{:S(2)}) collective-permute-start(bf16[2,1280,128]{1,2,0:T(8,128)(2,1)S(1)} %bitcast.51), channel_id=1, source_target_pairs={{4,0},{8,4},{12,8},{16,12},{20,16},{24,20},{28,24},{5,1},{9,5},{13... | collective-permute-start | bytes 1966088 | tf_op jit(solution)/shard_map/ppermute | solution.py:18
  31.8 0.6 dynamic-slice
  33.1 0.2 dynamic-update-slice
  33.3 0.2 dynamic-update-slice.1
  33.6 5.9 %all-reduce.3 = (f32[256]{0:T(256)S(1)}, f32[256]{0:T(256)S(1)}) all-reduce(f32[256]{0:T(256)S(1)} %dynamic-update-slice, f32[256]{0:T(256)S(1)} %dynamic-update-slice.1), channel_id=1, replica_groups=mesh['depth'=8,'filt'=4] {'filt'}, use_global_device_ids=true, to_apply=%add.1 | all-reduce | flops 512 | bytes 4096
  39.6 1.1 concatenate.11
  40.6 0.9 copy.25
  41.5 15.5 %collective-permute-done = bf16[2,1280,128]{1,2,0:T(8,128)(2,1)} collective-permute-done((bf16[2,1280,128]{1,2,0:T(8,128)(2,1)S(1)}, bf16[2,1280,128]{1,2,0:T(8,128)(2,1)}, u32[]{:S(2)}, u32[]{:S(2)}) %collective-permute-start) | collective-permute-done | bytes 655392 | tf_op jit(solution)/shard_map/ppermute | solution.py:17
  57.0 1.4 %copy.23 = bf16[2,1280,128]{2,1,0:T(8,128)(2,1)S(1)} copy(bf16[2,1280,128]{1,2,0:T(8,128)(2,1)} %collective-permute-done) | data formatting | bytes 1310720 | tf_op jit(solution)/shard_map/ppermute | solution.py:17
  58.5 0.3 copy.24
  58.8 0.2 maximum_bitcast_fusion
  59.0 1.3 %copy.34 = bf16[6,20,1,64,128]{4,1,3,0,2:T(8,128)(2,1)S(1)} copy(bf16[6,20,1,64,128]{4,3,1,0,2:T(8,128)(2,1)S(1)} %maximum_bitcast_fusion) | data formatting | bytes 3932160
  60.3 0.5 pad.5.clone
  60.8 0.3 copy.28
  61.1 0.1 slice.22
  61.3 0.2 copy-done.4
  61.5 12.9 %select_bitcast_fusion = bf16[4,18,1,8,9,256]{5,3,4,1,0,2:T(8,128)(2,1)S(1)} fusion(pred[8,9]{0,1:T(8,128)(4,1)S(1)} %copy-done.4, f32[256]{0:T(256)S(1)} %get-tuple-element.5, bf16[3,3,3,256,128]{4,3,2,1,0:T(8,128)(2,1)} %all-gather.3.cloned.1.call-done, bf16[6,20,1,7,2,128]{5,3,4,1,0,2:T(8,128)(2,1)S(1)} %slice.22, ...), kind=kOutput, calls=%fused_computation.25 | convolution fusion | flops 9191669760 | bytes 7066768 | tf_op jit(solution)/shard_map/conv_general_dilated | solution.py:31
  74.4 1.5 %copy-done = bf16[4,18,1,8,9,256]{5,3,4,1,0,2:T(8,128)(2,1)} copy-done((bf16[4,18,1,8,9,256]{5,3,4,1,0,2:T(8,128)(2,1)}, bf16[4,18,1,8,9,256]{5,3,4,1,0,2:T(8,128)(2,1)S(1)}, u32[]{:S(2)}) %copy-start) | copy-done | bytes 2654232
  76.0 12.6 %fusion.7 = f32[2,16,8,9,256]{4,2,3,1,0:T(8,128)S(1)} fusion(bf16[3,3,3,256,256]{4,3,2,1,0:T(8,128)(2,1)} %all-gather.5.cloned.1.call-done, bf16[4,18,1,7,1,256]{5,3,4,1,0,2:T(8,128)(2,1)S(1)} %get-tuple-element.8, bf16[4,18,1,7,1,256]{5,3,4,1,0,2:T(8,128)(2,1)S(1)} %get-tuple-element.7, bf16[4,18,1,8,9,256]{5,3,4,1,0,2:T(8,128)(2,1)} %copy-done), kind=kOutput, calls=%fused_computation.12 | convolution fusion | flops 8169947136 | bytes 9068544 | tf_op jit(solution)/shard_map/conv_general_dilated | solution.py:31
  88.6 0.7 copy.29
  89.3 0.2 slice.25
  89.5 1.2 %copy.30 = f32[2,16,1,64,256]{4,3,1,0,2:T(8,128)S(1)} copy(f32[2,16,1,64,256]{4,1,3,0,2:T(8,128)S(1)} %slice.25) | data formatting | bytes 4194304 | tf_op jit(solution)/shard_map/conv_general_dilated | solution.py:31
  90.7 0.3 fusion.30
  91.1 1.1 copy.31
  92.2 16.9 %all_to_all.24 = bf16[2,256,1024]{2,0,1:T(2,128)(2,1)S(1)} all-to-all(bf16[2,256,1024]{2,0,1:T(2,128)(2,1)S(1)} %copy.31), channel_id=1, replica_groups=mesh['depth'=8,'filt'=4] {'filt'}, dimensions={1} | all-to-all | bytes 2097152 | tf_op jit(solution)/shard_map/all_to_all | solution.py:72
  109.1 0.3 copy.32
  109.3 1.1 copy.35
  (21 shorter events, 0.4 us)
Async XLA Ops:
  6.5 54.7 %all-gather.3.cloned.1.call-start = ((), (), s32[]{:S(2)}) async-start(), calls=%async_computation.2 | async-start | bytes 2211840 | tf_op jit(solution)/shard_map/all_gather | solution.py:57
  7.3 68.8 %all-gather.5.cloned.1.call-start = ((), (), s32[]{:S(2)}) async-start(), calls=%async_computation.3 | async-start | bytes 4423680 | tf_op jit(solution)/shard_map/all_gather | solution.py:58
  8.0 23.8 %copy-start.3 = (u32[32]{0:T(128)S(1)}, u32[32]{0:T(128)}, u32[]{:S(2)}) copy-start(u32[32]{0:T(128)} %constant.47) | copy-start | bytes 388
  8.0 25.1 %copy-start.1 = (f32[64]{0:T(128)S(1)}, f32[64]{0:T(128)}, u32[]{:S(2)}) copy-start(f32[64]{0:T(128)} %param.7) | copy-start | bytes 772
  8.0 25.3 %copy-start.2 = (f32[64]{0:T(128)S(1)}, f32[64]{0:T(128)}, u32[]{:S(2)}) copy-start(f32[64]{0:T(128)} %param.9) | copy-start | bytes 772
  26.2 30.8 %collective-permute-start = (bf16[2,1280,128]{1,2,0:T(8,128)(2,1)S(1)}, bf16[2,1280,128]{1,2,0:T(8,128)(2,1)}, u32[]{:S(2)}, u32[]{:S(2)}) collective-permute-start(bf16[2,1280,128]{1,2,0:T(8,128)(2,1)S(1)} %bitcast.50), channel_id=1, source_target_pairs={{0,4},{4,8},{8,12},{12,16},{16,20},{20,24},{24,28},{1,5},{5,9},{9,... | collective-permute-start | bytes 1966088 | tf_op jit(solution)/shard_map/ppermute | solution.py:17
  30.5 27.9 %collective-permute-start.1 = (bf16[2,1280,128]{1,2,0:T(8,128)(2,1)S(1)}, bf16[2,1280,128]{1,2,0:T(8,128)(2,1)S(1)}, u32[]{:S(2)}, u32[]{:S(2)}) collective-permute-start(bf16[2,1280,128]{1,2,0:T(8,128)(2,1)S(1)} %bitcast.51), channel_id=1, source_target_pairs={{4,0},{8,4},{12,8},{16,12},{20,16},{24,20},{28,24},{5,1},{9,5},{13... | collective-permute-start | bytes 1966088 | tf_op jit(solution)/shard_map/ppermute | solution.py:18
  60.8 0.7 copy-start.4
  74.4 1.5 %copy-start = (bf16[4,18,1,8,9,256]{5,3,4,1,0,2:T(8,128)(2,1)}, bf16[4,18,1,8,9,256]{5,3,4,1,0,2:T(8,128)(2,1)S(1)}, u32[]{:S(2)}) copy-start(bf16[4,18,1,8,9,256]{5,3,4,1,0,2:T(8,128)(2,1)S(1)} %select_bitcast_fusion) | copy-start | bytes 7962628
Sparse Core Ops, SparseCore 0:
  8.9 25.7 all-gather.2
  36.2 30.9 all-gather.4
where the time goes:
time: 118 us; the launch traced here: 117 us
  blocking collectives  39.6 us (34%)
  matrix products  25.5 us (22%)
  waiting for transfers between devices  16.9 us (14%)
  local copies, waits for them, and re-layouts  14.5 us (12%)
  between operations  14.3 us (12%)
  starting transfers between devices  5.67 us (5%)
    conv_general_dilated x2, matrix products, convolve(): lax.conv_general_dilated(volume[None], kernel, (1, 1, 1), ((0, 0), (0, 0)...  25.5 us
    all_to_all x1, blocking collectives, local(): return lax.all_to_all(flat, 'filt', 1, 2, tiled=True)  16.9 us
    all_to_all x1, blocking collectives, local(): blocks = lax.all_to_all(row_blocks(features, parts, rows), 'filt', 0, 0)  16.8 us
    ppermute x1, waiting for transfers between devices, depth_padded(): low = lax.ppermute(block[block.shape[0] - width:], 'depth', forward)  15.5 us
    unnamed x1, blocking collectives  5.93 us
    ppermute x1, starting transfers between devices, depth_padded(): low = lax.ppermute(block[block.shape[0] - width:], 'depth', forward)  4.35 us
    unnamed x16, local copies, waits for them, and re-layouts  4.1 us
    conv_general_dilated x5, local copies, waits for them, and re-layouts, convolve(): lax.conv_general_dilated(volume[None], kernel, (1, 1, 1), ((0, 0), (0, 0)...  2.51 us
  transfers between devices with their start and end apart: 4, of which 1 were waited for; matrix products, arithmetic and copies ran while one was open for 18% of the time, Pallas kernels for 0%

commit v1 on v0

--- a/solution.py
+++ b/solution.py
@@ -5,6 +5,7 @@
 
 SIDE = 64
 REACH = 2
+PAIR = 2
 
 
 leak_slope = 0.3
@@ -12,11 +13,30 @@
 
 def depth_padded(block, width):
     count = lax.axis_size("depth")
-    forward = [(i, i + 1) for i in range(count - 1)]
+    forward = [(i, i + PAIR) for i in range(count - PAIR)]
     backward = [(target, source) for source, target in forward]
     low = lax.ppermute(block[block.shape[0] - width :], "depth", forward)
     high = lax.ppermute(block[:width], "depth", backward)
     return jnp.concatenate([low, block, high], axis=0)
+
+
+def gathered(block):
+    count = lax.axis_size("filt")
+    place = lax.axis_index("filt")
+    stride = count // 2
+    block = block[None]
+    while stride:
+        other = lax.ppermute(block, "filt", [(i, i ^ stride) for i in range(count)])
+        upper = (place // stride) % 2 == 1
+        block = jnp.where(upper, jnp.stack([other, block], 1), jnp.stack([block, other], 1))
+        block = block.reshape((-1,) + block.shape[2:])
+        stride //= 2
+    return block
+
+
+def whole_kernel(kernel):
+    blocks = gathered(kernel.reshape(27, kernel.shape[3], kernel.shape[4]))
+    return jnp.transpose(blocks, (1, 0, 2, 3)).reshape(3, 3, 3, -1, kernel.shape[4])
 
 
 def row_blocks(features, parts, rows):
@@ -49,27 +69,38 @@
 
 
 def local(features, first_kernel, first_bias, second_kernel, second_bias):
-    parts = lax.axis_size("filt")
+    shares = lax.axis_size("filt")
+    parts = PAIR * shares
     rows = SIDE // parts
-    planes, share = features.shape[0], features.shape[1]
-    channels = share * parts
-    depth_limit = planes * lax.axis_size("depth")
-    first_whole = lax.all_gather(first_kernel, "filt", axis=3, tiled=True)
-    second_whole = lax.all_gather(second_kernel, "filt", axis=3, tiled=True)
-    first_shift = lax.all_gather(first_bias, "filt", axis=0, tiled=True)
-    second_shift = lax.all_gather(second_bias, "filt", axis=0, tiled=True)
-    blocks = lax.all_to_all(row_blocks(features, parts, rows), "filt", 0, 0)
-    mine = jnp.transpose(blocks, (1, 3, 0, 2)).reshape(planes, -1, channels)
+    share = features.shape[1]
+    planes = features.shape[0] * PAIR
+    channels = share * shares
+    count = lax.axis_size("depth")
+    depth_limit = features.shape[0] * count
+    groups = [list(range(i * parts, (i + 1) * parts)) for i in range(count // PAIR)]
+    where = lax.axis_index("depth")
+    part = (where % PAIR) * shares + lax.axis_index("filt")
+    first_whole = whole_kernel(first_kernel)
+    second_whole = whole_kernel(second_kernel)
+    shifts = gathered(jnp.stack([first_bias, second_bias]))
+    first_shift, second_shift = shifts[:, 0].reshape(-1), shifts[:, 1].reshape(-1)
+    blocks = lax.all_to_all(
+        row_blocks(features, parts, rows), ("depth", "filt"), 0, 0, axis_index_groups=groups
+    )
+    blocks = blocks.reshape(PAIR, shares, features.shape[0], share, -1)
+    mine = jnp.transpose(blocks, (0, 2, 4, 1, 3)).reshape(planes, -1, channels)
     volume = depth_padded(mine, REACH).reshape(planes + 2 * REACH, rows + 2 * REACH, SIDE, channels)
     first_sum = convolve(volume, first_whole)
     hidden = activate(first_sum, first_shift)
-    deep = inside(planes + 2, lax.axis_index("depth") * planes - 1, depth_limit)
-    high = inside(rows + 2, lax.axis_index("filt") * rows - 1, SIDE)
+    deep = inside(planes + 2, (where // PAIR) * planes - 1, depth_limit)
+    high = inside(rows + 2, part * rows - 1, SIDE)
     usable = deep[:, None] & high[None, :]
     hidden = jnp.where(usable[:, :, None, None], hidden, 0.0).astype(jnp.bfloat16)
     activated = activate(convolve(hidden, second_whole), second_shift).astype(jnp.bfloat16)
-    flat = jnp.transpose(activated.reshape(planes, rows * SIDE, -1), (0, 2, 1))
-    return lax.all_to_all(flat, "filt", 1, 2, tiled=True)
+    flat = activated.reshape(PAIR, features.shape[0], rows * SIDE, shares, -1)
+    flat = jnp.transpose(flat, (0, 3, 1, 4, 2)).reshape(parts, features.shape[0], -1, rows * SIDE)
+    flat = lax.all_to_all(flat, ("depth", "filt"), 0, 0, axis_index_groups=groups)
+    return jnp.transpose(flat, (1, 2, 0, 3)).reshape(features.shape[0], -1, SIDE * SIDE)
 
 
 def solution(mesh):

time: 118 us -> 124 us (1.051)
  local copies, waits for them, and re-layouts: 14.5 us -> 37.7 us
  blocking collectives: 39.6 us -> 18 us
  other arithmetic: 0.72 us -> 17.2 us
  between operations: 14.3 us -> 0.27 us
  starting transfers between devices: 5.67 us -> 15 us
  matrix products: 25.5 us -> 19.1 us
    all_to_all x2 -> x1, blocking collectives: 33.7 us -> 18 us  [local(): lax.all_to_all(flat, ('depth', 'filt'), 0, 0, axis_index_groups=groups)]
    ppermute x1, waiting for transfers between devices: 15.5 us -> 0.01 us  [depth_padded(): low = lax.ppermute(block[block.shape[0] - width:], 'depth', forward)]
    unnamed x16 -> x18, local copies, waits for them, and re-layouts: 4.1 us -> 17.1 us
    select_n x0 -> x9, other arithmetic: none -> 12.5 us  [gathered(): jnp.where(upper, jnp.stack([other, block], 1), jnp.stack([block, other], 1))]
    all_to_all x0 -> x1, waiting for transfers between devices: none -> 8.36 us  [local(): lax.all_to_all(row_blocks(features, parts, rows), ('depth', 'filt'), 0, 0...]
    ppermute x0 -> x6, waiting for transfers between devices: none -> 7.67 us  [gathered(): other = lax.ppermute(block, 'filt', [(i, i ^ stride) for i in range(count)])]
    conv_general_dilated x2, matrix products: 25.5 us -> 19.1 us  [convolve(): lax.conv_general_dilated(volume[None], kernel, (1, 1, 1), ((0, 0), (0, 0)...]
    unnamed x1 -> x0, blocking collectives: 5.93 us -> none
  transfers between devices with their start and end apart: 4 -> 9, of which waited for: 1 -> 3; matrix products, arithmetic and copies ran while one was open for 18% -> 41% of each run, Pallas kernels for 0% -> 0%
where the time goes in v1:
time: 124 us; the launch traced here: 123 us
  local copies, waits for them, and re-layouts  37.7 us (30%)
  matrix products  19.1 us (15%)
  blocking collectives  18 us (15%)
  other arithmetic  17.2 us (14%)
  waiting for transfers between devices  16 us (13%)
  starting transfers between devices  15 us (12%)
    conv_general_dilated x2, matrix products, convolve(): lax.conv_general_dilated(volume[None], kernel, (1, 1, 1), ((0, 0), (0, 0)...  19.1 us
    all_to_all x1, blocking collectives, local(): lax.all_to_all(flat, ('depth', 'filt'), 0, 0, axis_index_groups=groups)  18 us
    unnamed x18, local copies, waits for them, and re-layouts  17.1 us
    select_n x9, other arithmetic, gathered(): jnp.where(upper, jnp.stack([other, block], 1), jnp.stack([block, other], 1))  12.5 us
    all_to_all x1, waiting for transfers between devices, local(): lax.all_to_all(row_blocks(features, parts, rows), ('depth', 'filt'), 0, 0...  8.36 us
    ppermute x6, waiting for transfers between devices, gathered(): other = lax.ppermute(block, 'filt', [(i, i ^ stride) for i in range(count)])  7.67 us
    concatenate x4, local copies, waits for them, and re-layouts, depth_padded(): return jnp.concatenate([low, block, high], axis=0)  5.4 us
    ppermute x6, starting transfers between devices, gathered(): other = lax.ppermute(block, 'filt', [(i, i ^ stride) for i in range(count)])  5.32 us
  transfers between devices with their start and end apart: 9, of which 3 were waited for; matrix products, arithmetic and copies ran while one was open for 41% of the time, Pallas kernels for 0%

profile of v1, /device:TPU:0, one launch (start us, length us, event | category | flops | bytes accessed | tf_op | source)
XLA Modules:
  0.0 123.4 jit_solution(8138503184124107589)
XLA Ops:
  0.0 2.9 %collective-permute-start.2 = (bf16[1,27,64,128]{3,2,1,0:T(8,128)(2,1)}, bf16[1,27,64,128]{3,2,1,0:T(8,128)(2,1)S(1)}, u32[]{:S(2)}, u32[]{:S(2)}) collective-permute-start(bf16[1,27,64,128]{3,2,1,0:T(8,128)(2,1)} %bitcast.100), channel_id=1, source_target_pairs={{0,2},{1,3},{2,0},{3,1},{4,6},{5,7},{6,4},{7,5},{8,10},{9,11},{10,... | collective-permute-start | bytes 1327112 | tf_op jit(solution)/shard_map/ppermute | solution.py:29
  3.7 1.5 %fusion.32 = bf16[8,2,32,768]{3,2,1,0:T(8,128)(2,1)} fusion(bf16[2,32,4096]{2,1,0:T(8,128)(2,1)} %param.5), kind=kLoop, calls=%fused_computation.41 | loop fusion | bytes 622592
  5.3 1.5 %bitcast_dynamic-update-slice_fusion.5 = bf16[8,2,32,768]{3,2,1,0:T(8,128)(2,1)} fusion(bf16[8,2,32,768]{3,2,1,0:T(8,128)(2,1)} %fusion.32, bf16[2,32,4096]{2,1,0:T(8,128)(2,1)} %param.5), kind=kLoop, calls=%fused_computation.49 | loop fusion | bytes 196608
  6.8 1.5 %bitcast_dynamic-update-slice_fusion.4 = bf16[8,2,32,768]{3,2,1,0:T(8,128)(2,1)} fusion(bf16[8,2,32,768]{3,2,1,0:T(8,128)(2,1)} %bitcast_dynamic-update-slice_fusion.5, bf16[2,32,4096]{2,1,0:T(8,128)(2,1)} %param.5), kind=kLoop, calls=%fused_computation.48 | loop fusion | bytes 196608
  8.3 1.5 %bitcast_dynamic-update-slice_fusion.3 = bf16[8,2,32,768]{3,2,1,0:T(8,128)(2,1)} fusion(bf16[8,2,32,768]{3,2,1,0:T(8,128)(2,1)} %bitcast_dynamic-update-slice_fusion.4, bf16[2,32,4096]{2,1,0:T(8,128)(2,1)} %param.5), kind=kLoop, calls=%fused_computation.47 | loop fusion | bytes 196608
  9.9 1.5 %bitcast_dynamic-update-slice_fusion.2 = bf16[8,2,32,768]{3,2,1,0:T(8,128)(2,1)} fusion(bf16[8,2,32,768]{3,2,1,0:T(8,128)(2,1)} %bitcast_dynamic-update-slice_fusion.3, bf16[2,32,4096]{2,1,0:T(8,128)(2,1)} %param.5), kind=kLoop, calls=%fused_computation.46 | loop fusion | bytes 196608
  11.4 1.5 %bitcast_dynamic-update-slice_fusion.1 = bf16[8,2,32,768]{3,2,1,0:T(8,128)(2,1)} fusion(bf16[8,2,32,768]{3,2,1,0:T(8,128)(2,1)} %bitcast_dynamic-update-slice_fusion.2, bf16[2,32,4096]{2,1,0:T(8,128)(2,1)} %param.5), kind=kLoop, calls=%fused_computation.45 | loop fusion | bytes 196608
  13.0 1.5 %bitcast_dynamic-update-slice_fusion = bf16[8,2,32,768]{3,2,1,0:T(8,128)(2,1)} fusion(bf16[8,2,32,768]{3,2,1,0:T(8,128)(2,1)} %bitcast_dynamic-update-slice_fusion.1, bf16[2,32,4096]{2,1,0:T(8,128)(2,1)} %param.5), kind=kLoop, calls=%fused_computation.44 | loop fusion | bytes 196608
  14.5 1.5 %fusion.34 = bf16[8,2,32,768]{3,2,1,0:T(8,128)(2,1)} fusion(bf16[8,2,32,768]{3,2,1,0:T(8,128)(2,1)} %bitcast_dynamic-update-slice_fusion, bf16[2,32,4096]{2,1,0:T(8,128)(2,1)} %param.5), kind=kLoop, calls=%fused_computation.43 | loop fusion | bytes 622592 | tf_op jit(solution)/shard_map/stack | solution.py:45
  16.0 4.1 %all-to-all-start = ((bf16[8,2,32,768]{3,2,1,0:T(8,128)(2,1)}), bf16[8,2,32,768]{3,2,1,0:T(8,128)(2,1)S(1)}, u32[]{:S(2)}, u32[]{:S(2)}) async-start(bf16[8,2,32,768]{3,2,1,0:T(8,128)(2,1)} %fusion.34), calls=%async_computation | async-start | bytes 1572864 | tf_op jit(solution)/shard_map/all_to_all | solution.py:87
  20.2 2.0 %collective-permute-start.6 = (bf16[1,27,64,256]{3,2,1,0:T(8,128)(2,1)S(1)}, bf16[1,27,64,256]{3,2,1,0:T(8,128)(2,1)}, u32[]{:S(2)}, u32[]{:S(2)}) collective-permute-start(bf16[1,27,64,256]{3,2,1,0:T(8,128)(2,1)S(1)} %bitcast.96), channel_id=1, source_target_pairs={{0,2},{1,3},{2,0},{3,1},{4,6},{5,7},{6,4},{7,5},{8,10},{9,11},{10,... | collective-permute-start | bytes 2654216 | tf_op jit(solution)/shard_map/ppermute | solution.py:29
  22.4 1.1 collective-permute-done.5
  24.9 8.4 %all-to-all-done = bf16[8,2,32,768]{3,2,1,0:T(8,128)(2,1)S(1)} async-done(((bf16[8,2,32,768]{3,2,1,0:T(8,128)(2,1)}), bf16[8,2,32,768]{3,2,1,0:T(8,128)(2,1)S(1)}, u32[]{:S(2)}, u32[]{:S(2)}) %all-to-all-start) | async-done | bytes 786464 | tf_op jit(solution)/shard_map/all_to_all | solution.py:87
  33.4 4.2 %collective-permute-start = (bf16[2,768,128]{1,2,0:T(8,128)(2,1)S(1)}, bf16[2,768,128]{1,2,0:T(8,128)(2,1)}, u32[]{:S(2)}, u32[]{:S(2)}) collective-permute-start(bf16[2,768,128]{1,2,0:T(8,128)(2,1)S(1)} %bitcast.106), channel_id=1, source_target_pairs={{0,8},{4,12},{8,16},{12,20},{16,24},{20,28},{1,9},{5,13},{9,17},{1... | collective-permute-start | bytes 1179656 | tf_op jit(solution)/shard_map/ppermute | solution.py:18
  38.4 1.3 %collective-permute-start.1 = (bf16[2,768,128]{1,2,0:T(8,128)(2,1)}, bf16[2,768,128]{1,2,0:T(8,128)(2,1)}, u32[]{:S(2)}, u32[]{:S(2)}) collective-permute-start(bf16[2,768,128]{1,2,0:T(8,128)(2,1)} %bitcast.13), channel_id=1, source_target_pairs={{8,0},{12,4},{16,8},{20,12},{24,16},{28,20},{9,1},{13,5},{17,9},{2... | collective-permute-start | bytes 1179656 | tf_op jit(solution)/shard_map/ppermute | solution.py:19
  41.7 2.7 %concatenate.71 = bf16[1,4,12,64,128]{3,2,4,1,0:T(8,128)(2,1)S(1)} reshape(bf16[2,2,768,4,32]{2,4,3,1,0:T(8,128)(2,1)} %copy.87) | data formatting | bytes 1572864 | tf_op jit(solution)/shard_map/concatenate | solution.py:20
  44.4 6.5 %collective-permute-done.6 = bf16[1,27,64,256]{3,2,1,0:T(8,128)(2,1)} collective-permute-done((bf16[1,27,64,256]{3,2,1,0:T(8,128)(2,1)S(1)}, bf16[1,27,64,256]{3,2,1,0:T(8,128)(2,1)}, u32[]{:S(2)}, u32[]{:S(2)}) %collective-permute-start.6) | collective-permute-done | bytes 884768 | tf_op jit(solution)/shard_map/ppermute | solution.py:29
  50.9 2.9 %maximum_select_fusion.2 = bf16[2,27,64,256]{3,2,1,0:T(8,128)(2,1)} fusion(bf16[1,27,64,256]{3,2,1,0:T(8,128)(2,1)S(1)} %bitcast.97, bf16[1,27,64,256]{3,2,1,0:T(8,128)(2,1)} %collective-permute-done.6, pred[]{:T(512)S(6)} %eq.19), kind=kLoop, calls=%fused_computation.31 | loop fusion | flops 2654208 | bytes 3538945 | tf_op jit(solution)/shard_map/jit(_where)/select_n | solution.py:31
  53.8 3.0 %maximum_select_fusion.3 = bf16[2,1,27,64,256]{4,3,2,1,0:T(8,128)(2,1)} fusion(bf16[1,1,27,64,256]{4,3,2,1,0:T(8,128)(2,1)S(1)} %bitcast.98, bf16[1,1,27,64,256]{4,3,2,1,0:T(8,128)(2,1)} %bitcast.40, pred[]{:T(512)S(6)} %eq.19), kind=kLoop, calls=%fused_computation.32 | loop fusion | flops 2654208 | bytes 3538945 | tf_op jit(solution)/shard_map/jit(_where)/select_n | solution.py:31
  56.9 1.2 copy.86
  58.9 1.2 copy.89
  60.1 1.7 %copy.91 = bf16[1,2,12,64,128]{3,2,4,1,0:T(8,128)(2,1)} copy(bf16[1,2,12,64,128]{4,3,2,1,0:T(8,128)(2,1)S(1)} %bitcast.105) | data formatting | bytes 786432 | tf_op jit(solution)/shard_map/concatenate | solution.py:20
  61.8 3.6 %maximum_bitcast_fusion = bf16[8,12,1,64,128]{3,1,4,0,2:T(8,128)(2,1)} fusion(bf16[1,2,12,64,128]{3,2,4,1,0:T(8,128)(2,1)} %copy.91, bf16[1,4,12,64,128]{3,2,4,1,0:T(8,128)(2,1)S(1)} %concatenate.71, bf16[1,2,12,64,128]{3,2,4,1,0:T(8,128)(2,1)S(1)} %copy.90), kind=kLoop, calls=%fused_computation.10 | loop fusion | flops 1572864 | bytes 3145728 | tf_op jit(solution)/shard_map/concatenate | solution.py:20
  65.4 5.0 %copy.106 = bf16[8,12,1,64,128]{4,0,3,1,2:T(8,128)(2,1)S(1)} copy(bf16[8,12,1,64,128]{3,1,4,0,2:T(8,128)(2,1)} %maximum_bitcast_fusion) | data formatting | bytes 3145728
  71.8 1.7 %maximum_select_fusion.1 = bf16[2,2,27,64,128]{4,3,2,1,0:T(8,128)(2,1)S(1)} fusion(bf16[2,1,27,64,128]{4,3,2,1,0:T(8,128)(2,1)S(1)} %copy-done.1, bf16[2,1,27,64,128]{4,3,2,1,0:T(8,128)(2,1)} %bitcast.19, pred[]{:T(512)S(6)} %eq.18), kind=kLoop, calls=%fused_computation.30 | loop fusion | flops 2654208 | bytes 3538945 | tf_op jit(solution)/shard_map/jit(_where)/select_n | solution.py:31
  74.2 9.3 %fusion.17 = bf16[6,10,1,8,9,256]{5,3,4,1,0,2:T(8,128)(2,1)S(1)} fusion(f32[256]{0:T(256)S(1)} %add.74, pred[8,9]{0,1:T(8,128)(4,1)S(1)} %copy-done.4, pred[6,10]{1,0:T(8,128)(4,1)S(1)} %broadcast_and_fusion, bf16[3,3,3,256,128]{4,3,2,1,0:T(8,128)(2,1)S(1)} %bitcast.99, bf16[8,12,1,7,2,128]{5,3,4,1,0,2:T(8,128)(2,1)S(1)} %slice.68, ...), kind=kOutput, calls=%fused_computation.22 | convolution fusion | flops 7659454464 | bytes 6096004 | tf_op jit(solution)/shard_map/conv_general_dilated | solution.py:51
  83.6 2.7 %maximum_select_fusion = bf16[2,2,27,64,256]{4,3,2,1,0:T(8,128)(2,1)S(1)} fusion(bf16[2,1,27,64,256]{4,3,2,1,0:T(8,128)(2,1)S(1)} %copy-done, bf16[2,1,27,64,256]{4,3,2,1,0:T(8,128)(2,1)} %bitcast.39, pred[]{:T(512)S(6)} %eq.18), kind=kLoop, calls=%fused_computation.11 | loop fusion | flops 5308416 | bytes 7077889 | tf_op jit(solution)/shard_map/jit(_where)/select_n | solution.py:31
  86.8 9.8 %fusion.7 = f32[4,8,8,9,256]{4,2,3,1,0:T(8,128)S(1)} fusion(bf16[3,3,3,256,256]{4,3,2,1,0:T(8,128)(2,1)S(1)} %bitcast.95, bf16[6,10,1,7,1,256]{5,3,4,1,0,2:T(8,128)(2,1)S(1)} %get-tuple-element.6, bf16[6,10,1,7,1,256]{5,3,4,1,0,2:T(8,128)(2,1)S(1)} %get-tuple-element.5, bf16[6,10,1,8,9,256]{5,3,4,1,0,2:T(8,128)(2,1)S(1)} %fusion.17), kind=kOutput, calls=%fused_computation.14 | convolution fusion | flops 8167243776 | bytes 8540160 | tf_op jit(solution)/shard_map/conv_general_dilated | solution.py:51
  97.5 2.9 %copy.103 = f32[4,8,1,64,256]{3,1,4,0,2:T(8,128)} copy(f32[4,8,1,64,256]{4,1,3,0,2:T(8,128)S(1)} %slice.72) | data formatting | bytes 4194304 | tf_op jit(solution)/shard_map/conv_general_dilated | solution.py:51
  100.4 3.4 %squeeze.4 = f32[2,2,512,4,64]{2,4,3,1,0:T(8,128)S(1)} reshape(f32[4,8,1,64,256]{3,1,4,0,2:T(8,128)} %copy.103) | data formatting | bytes 4194304 | tf_op jit(solution)/shard_map/squeeze | solution.py:51
  104.3 18.0 %all_to_all.10 = bf16[8,2,64,512]{3,2,1,0:T(8,128)(2,1)S(1)} all-to-all(bf16[8,2,64,512]{3,2,1,0:T(8,128)(2,1)S(1)} %bitcast.93), channel_id=1, replica_groups={{0,1,2,3,4,5,6,7},{8,9,10,11,12,13,14,15},{16,17,18,19,20,21,22,23},{24..., dimensions={0} | all-to-all | bytes 2097152 | tf_op jit(solution)/shard_map/all_to_all | solution.py:102
  122.3 1.1 copy.107
  (47 shorter events, 9.8 us)
Async XLA Ops:
  0.0 23.7 %copy-start.3 = (bf16[3,3,3,64,128]{4,3,2,1,0:T(8,128)(2,1)S(1)}, bf16[3,3,3,64,128]{4,3,2,1,0:T(8,128)(2,1)}, u32[]{:S(2)}) copy-start(bf16[3,3,3,64,128]{4,3,2,1,0:T(8,128)(2,1)} %param.6) | copy-start | bytes 1327108
  0.0 20.2 %copy-start.2 = (bf16[3,3,3,64,256]{4,3,2,1,0:T(8,128)(2,1)S(1)}, bf16[3,3,3,64,256]{4,3,2,1,0:T(8,128)(2,1)}, u32[]{:S(2)}) copy-start(bf16[3,3,3,64,256]{4,3,2,1,0:T(8,128)(2,1)} %param.8) | copy-start | bytes 2654212
  0.0 23.7 %collective-permute-start.2 = (bf16[1,27,64,128]{3,2,1,0:T(8,128)(2,1)}, bf16[1,27,64,128]{3,2,1,0:T(8,128)(2,1)S(1)}, u32[]{:S(2)}, u32[]{:S(2)}) collective-permute-start(bf16[1,27,64,128]{3,2,1,0:T(8,128)(2,1)} %bitcast.100), channel_id=1, source_target_pairs={{0,2},{1,3},{2,0},{3,1},{4,6},{5,7},{6,4},{7,5},{8,10},{9,11},{10,... | collective-permute-start | bytes 1327112 | tf_op jit(solution)/shard_map/ppermute | solution.py:29
  3.6 18.7 %collective-permute-start.4 = (f32[1,2,64]{2,1,0:T(2,128)S(1)}, f32[1,2,64]{2,1,0:T(2,128)S(1)}, u32[]{:S(2)}, u32[]{:S(2)}) collective-permute-start(f32[1,2,64]{2,1,0:T(2,128)S(1)} %get-tuple-element.11), channel_id=1, source_target_pairs={{0,2},{1,3},{2,0},{3,1},{4,6},{5,7},{6,4},{7,5},{8,10},{9,11},{10,... | collective-permute-start | bytes 1544 | tf_op jit(solution)/shard_map/ppermute | solution.py:29
  16.0 17.2 %all-to-all-start = ((bf16[8,2,32,768]{3,2,1,0:T(8,128)(2,1)}), bf16[8,2,32,768]{3,2,1,0:T(8,128)(2,1)S(1)}, u32[]{:S(2)}, u32[]{:S(2)}) async-start(bf16[8,2,32,768]{3,2,1,0:T(8,128)(2,1)} %fusion.34), calls=%async_computation | async-start | bytes 1572864 | tf_op jit(solution)/shard_map/all_to_all | solution.py:87
  20.2 30.8 %collective-permute-start.6 = (bf16[1,27,64,256]{3,2,1,0:T(8,128)(2,1)S(1)}, bf16[1,27,64,256]{3,2,1,0:T(8,128)(2,1)}, u32[]{:S(2)}, u32[]{:S(2)}) collective-permute-start(bf16[1,27,64,256]{3,2,1,0:T(8,128)(2,1)S(1)} %bitcast.96), channel_id=1, source_target_pairs={{0,2},{1,3},{2,0},{3,1},{4,6},{5,7},{6,4},{7,5},{8,10},{9,11},{10,... | collective-permute-start | bytes 2654216 | tf_op jit(solution)/shard_map/ppermute | solution.py:29
  22.3 1.2 collective-permute-start.5
  24.7 46.2 %collective-permute-start.3 = (bf16[2,27,64,128]{3,2,1,0:T(8,128)(2,1)}, bf16[2,27,64,128]{3,2,1,0:T(8,128)(2,1)}, u32[]{:S(2)}, u32[]{:S(2)}) collective-permute-start(bf16[2,27,64,128]{3,2,1,0:T(8,128)(2,1)} %maximum_select_fusion.4), channel_id=1, source_target_pairs={{0,1},{1,0},{2,3},{3,2},{4,5},{5,4},{6,7},{7,6},{8,9},{9,8},{10,11... | collective-permute-start | bytes 2654216 | tf_op jit(solution)/shard_map/ppermute | solution.py:29
  33.4 23.5 %collective-permute-start = (bf16[2,768,128]{1,2,0:T(8,128)(2,1)S(1)}, bf16[2,768,128]{1,2,0:T(8,128)(2,1)}, u32[]{:S(2)}, u32[]{:S(2)}) collective-permute-start(bf16[2,768,128]{1,2,0:T(8,128)(2,1)S(1)} %bitcast.106), channel_id=1, source_target_pairs={{0,8},{4,12},{8,16},{12,20},{16,24},{20,28},{1,9},{5,13},{9,17},{1... | collective-permute-start | bytes 1179656 | tf_op jit(solution)/shard_map/ppermute | solution.py:18
  38.4 20.5 %collective-permute-start.1 = (bf16[2,768,128]{1,2,0:T(8,128)(2,1)}, bf16[2,768,128]{1,2,0:T(8,128)(2,1)}, u32[]{:S(2)}, u32[]{:S(2)}) collective-permute-start(bf16[2,768,128]{1,2,0:T(8,128)(2,1)} %bitcast.13), channel_id=1, source_target_pairs={{8,0},{12,4},{16,8},{20,12},{24,16},{28,20},{9,1},{13,5},{17,9},{2... | collective-permute-start | bytes 1179656 | tf_op jit(solution)/shard_map/ppermute | solution.py:19
  53.8 29.8 %collective-permute-start.7 = (bf16[2,27,64,256]{3,2,1,0:T(8,128)(2,1)}, bf16[2,27,64,256]{3,2,1,0:T(8,128)(2,1)}, u32[]{:S(2)}, u32[]{:S(2)}) collective-permute-start(bf16[2,27,64,256]{3,2,1,0:T(8,128)(2,1)} %maximum_select_fusion.2), channel_id=1, source_target_pairs={{0,1},{1,0},{2,3},{3,2},{4,5},{5,4},{6,7},{7,6},{8,9},{9,8},{10,11... | collective-permute-start | bytes 5308424 | tf_op jit(solution)/shard_map/ppermute | solution.py:29
  70.6 1.2 copy-start.1
  73.5 0.7 copy-start.4
  74.2 9.4 %copy-start = (bf16[2,1,27,64,256]{4,3,2,1,0:T(8,128)(2,1)S(1)}, bf16[2,1,27,64,256]{4,3,2,1,0:T(8,128)(2,1)}, u32[]{:S(2)}) copy-start(bf16[2,1,27,64,256]{4,3,2,1,0:T(8,128)(2,1)} %maximum_select_fusion.3) | copy-start | bytes 5308420

commit v2 on v0

v2 whole, which is shorter than its diff:
```python
import functools

import jax
import jax.numpy as jnp
from jax import lax
from jax.experimental import pallas as pl
from jax.experimental.pallas import tpu as pltpu
from jax.sharding import PartitionSpec as P

SIDE = 64
REACH = 2
PAIR = 2
MESH = pl.DeviceIdType.MESH


leak_slope = 0.3


def activate(summed, bias):
    shifted = summed + bias
    return jnp.where(shifted > 0, shifted, leak_slope * shifted)


def spread(values, buffer, plane):
    cells, channels = values.shape
    column = lax.broadcasted_iota(jnp.int32, (cells, 1), 0) % SIDE
    before = jnp.where(column > 0, pltpu.roll(values, 1, 0), 0.0)
    after = jnp.where(column < SIDE - 1, pltpu.roll(values, cells - 1, 0), 0.0)
    buffer[plane, :, 0:channels] = before.astype(jnp.bfloat16)
    buffer[plane, :, channels : 2 * channels] = values.astype(jnp.bfloat16)
    buffer[plane, :, 2 * channels : 3 * channels] = after.astype(jnp.bfloat16)


def tap_sum(buffer, kernels, shares, plane, cells):
    total = None
    for tap_d in range(3):
        for tap_h in range(3):
            window = buffer[plane + tap_d, tap_h * SIDE : tap_h * SIDE + cells, :]
            weights = jnp.concatenate(
                [kernels[i, 3 * tap_d + tap_h] for i in range(shares)], axis=0
            )
            term = lax.dot_general(
                window, weights, (((1,), (1,)), ((), ())), preferred_element_type=jnp.float32
            )
            total = term if total is None else total + term
    return total


def kernel(
    shares, count, depth_planes,
    x_ref, k1_ref, k2_ref, b_ref, out_ref,
    held, taps1, taps2, k1_all, k2_all, b_all, results,
    x_send, x_recv, z_send, z_recv, w_send, w_recv, b_send, b_recv, o_send, o_recv, own_sem,
):
    parts = PAIR * shares
    rows = SIDE // parts
    span = (rows + 2 * REACH) * SIDE
    planes = PAIR * depth_planes
    where = lax.axis_index("depth")
    f = lax.axis_index("filt")
    base = (where // PAIR) * PAIR
    side = where % PAIR
    part = side * shares + f
    mate = f + 1 - 2 * (f % 2)
    below = where >= PAIR
    above = where < count - PAIR

    def home(other):
        return (base + other // shares, other % shares)

    barrier = pltpu.get_barrier_semaphore()
    for k in range(1, parts):
        pl.semaphore_signal(barrier, inc=1, device_id=home((part + k) % parts), device_id_type=MESH)

    @pl.when(below)
    def _():
        pl.semaphore_signal(barrier, inc=1, device_id=(where - PAIR, f), device_id_type=MESH)

    @pl.when(above)
    def _():
        pl.semaphore_signal(barrier, inc=1, device_id=(where + PAIR, f), device_id_type=MESH)

    pl.semaphore_wait(barrier, parts - 1 + below.astype(jnp.int32) + above.astype(jnp.int32))

    def x_copy(k):
        to = (part + k) % parts
        return pltpu.make_async_remote_copy(
            src_ref=x_ref.at[:, :, pl.ds(pl.multiple_of(to * rows * SIDE, 128), span)],
            dst_ref=held.at[1 + side, f],
            send_sem=x_send.at[k], recv_sem=x_recv.at[k],
            device_id=home(to), device_id_type=MESH,
        )

    def w_first(layer, ref, dest, m):
        to = mate if m == 0 else (f + 2 * m) % shares
        return pltpu.make_async_remote_copy(
            src_ref=ref, dst_ref=dest.at[f],
            send_sem=w_send.at[layer, 0, m], recv_sem=w_recv.at[layer, 0, m],
            device_id=(where, to), device_id_type=MESH,
        )

    def w_second(layer, dest, m):
        source = (f - 2 * m + shares) % shares
        return pltpu.make_async_remote_copy(
            src_ref=dest.at[source], dst_ref=dest.at[source],
            send_sem=w_send.at[layer, 1, m], recv_sem=w_recv.at[layer, 1, m],
            device_id=(where, mate), device_id_type=MESH,
        )

    def b_copy(k):
        return pltpu.make_async_remote_copy(
            src_ref=b_ref, dst_ref=b_all.at[f], send_sem=b_send.at[k], recv_sem=b_recv.at[k],
            device_id=(where, (f + k) % shares), device_id_type=MESH,
        )

    chips = shares // 2
    x_copies = [x_copy(k) for k in range(1, parts)]
    first1 = [w_first(0, k1_ref, k1_all, m) for m in range(chips)]
    first2 = [w_first(1, k2_ref, k2_all, m) for m in range(chips)]
    second1 = [w_second(0, k1_all, m) for m in range(1, chips)]
    second2 = [w_second(1, k2_all, m) for m in range(1, chips)]
    b_copies = [b_copy(k) for k in range(1, shares)]
    own = [
        pltpu.make_async_copy(
            x_ref.at[:, :, pl.ds(pl.multiple_of(part * rows * SIDE, 128), span)],
            held.at[1 + side, f], own_sem.at[0],
        ),
        pltpu.make_async_copy(k1_ref, k1_all.at[f], own_sem.at[1]),
        pltpu.make_async_copy(k2_ref, k2_all.at[f], own_sem.at[2]),
        pltpu.make_async_copy(b_ref, b_all.at[f], own_sem.at[3]),
    ]
    for copy in x_copies + own + first1 + b_copies:
        copy.start()
    own[0].wait()
    for copy in x_copies:
        copy.wait_recv()

    def z_copy(up):
        return pltpu.make_async_remote_copy(
            src_ref=held.at[2 if up else 1], dst_ref=held.at[0 if up else 3],
            send_sem=z_send.at[int(up)], recv_sem=z_recv.at[int(up)],
            device_id=(where + PAIR if up else where - PAIR, f), device_id_type=MESH,
        )

    up_copy, down_copy = z_copy(True), z_copy(False)

    @pl.when(above)
    def _():
        up_copy.start()

    @pl.when(below)
    def _():
        down_copy.start()

    for copy in first2:
        copy.start()

    @pl.when(jnp.logical_not(below))
    def _():
        held[0] = jnp.zeros(held.shape[1:], held.dtype)

    @pl.when(jnp.logical_not(above))
    def _():
        held[3] = jnp.zeros(held.shape[1:], held.dtype)

    def turn(plane):
        block = jnp.concatenate(
            [held[plane // depth_planes, i, plane % depth_planes] for i in range(shares)], axis=0
        )
        spread(jnp.transpose(block.astype(jnp.float32)), taps1, plane)

    @pl.loop(depth_planes, 3 * depth_planes)
    def _(plane):
        turn(plane)

    for copy in first1:
        copy.wait_recv()
    for copy in second1:
        copy.start()

    @pl.when(below)
    def _():
        up_copy.wait_recv()

    @pl.when(above)
    def _():
        down_copy.wait_recv()

    @pl.loop(0, depth_planes)
    def _(plane):
        turn(plane)
        turn(plane + 3 * depth_planes)

    own[1].wait()
    own[3].wait()
    for copy in second1 + b_copies:
        copy.wait_recv()
    bias = jnp.sum(b_all[...], axis=0)
    wide = (rows + 2) * SIDE
    low_row = part * rows - 1
    low_plane = base * depth_planes - 1

    @pl.loop(0, planes + 2)
    def _(plane):
        hidden = activate(tap_sum(taps1, k1_all, shares, plane, wide), bias[0:1])
        row = low_row + lax.broadcasted_iota(jnp.int32, (wide, 1), 0) // SIDE
        deep = low_plane + plane
        usable = (row >= 0) & (row < SIDE) & (deep >= 0) & (deep < count * depth_planes)
        spread(jnp.where(usable, hidden, 0.0), taps2, plane)

    own[2].wait()
    for copy in first2:
        copy.wait_recv()
    for copy in second2:
        copy.start()
    for copy in second2:
        copy.wait_recv()
    cells = rows * SIDE
    share = results.shape[1] // shares

    def o_copy(plane, k):
        to = (f + k) % shares
        goal = (plane // depth_planes) * shares + to
        gap = (goal - part + parts) % parts
        level = plane % depth_planes
        lanes = pl.ds(pl.multiple_of(part * cells, 128), cells)
        source = results.at[plane, pl.ds(pl.multiple_of(to * share, share), share), :]
        remote = pltpu.make_async_remote_copy(
            src_ref=source, dst_ref=out_ref.at[level, :, lanes],
            send_sem=o_send.at[plane, k], recv_sem=o_recv.at[level, gap],
            device_id=home(goal), device_id_type=MESH,
        )
        local = pltpu.make_async_copy(source, out_ref.at[level, :, lanes], o_send.at[plane, k])
        return gap, remote, local

    @pl.loop(0, planes)
    def _(plane):
        done = activate(tap_sum(taps2, k2_all, shares, plane, cells), bias[1:2])
        results[plane] = jnp.transpose(done).astype(jnp.bfloat16)
        for k in range(shares):
            gap, remote, local = o_copy(plane, k)
            if k == 0:

                @pl.when(gap == 0)
                def _():
                    local.start()

                @pl.when(gap != 0)
                def _():
                    remote.start()

            else:
                remote.start()

    for level in range(depth_planes):
        for gap in range(1, parts):
            lanes = pl.ds(pl.multiple_of(((part - gap + parts) % parts) * cells, 128), cells)
            pltpu.make_async_remote_copy(
                src_ref=results.at[0, 0:share, :], dst_ref=out_ref.at[level, :, lanes],
                send_sem=o_send.at[0, 0], recv_sem=o_recv.at[level, gap],
                device_id=home((part + gap) % parts), device_id_type=MESH,
            ).wait_recv()
    for plane in range(planes):
        for k in range(shares):
            gap, remote, local = o_copy(plane, k)
            if k == 0:

                @pl.when(gap == 0)
                def _():
                    local.wait()

                @pl.when(gap != 0)
                def _():
                    remote.wait_send()

            else:
                remote.wait_send()
    for copy in x_copies + first1 + first2 + second1 + second2 + b_copies:
        copy.wait_send()

    @pl.when(above)
    def _():
        up_copy.wait_send()

    @pl.when(below)
    def _():
        down_copy.wait_send()


def joined(kernel_part):
    taps = kernel_part.reshape((9, 3) + kernel_part.shape[3:])
    return jnp.transpose(taps, (0, 2, 1, 3)).reshape(9, taps.shape[2], -1)


def local(features, first_kernel, first_bias, second_kernel, second_bias):
    shares = lax.axis_size("filt")
    count = lax.axis_size("depth")
    depth_planes, share, _ = features.shape
    parts = PAIR * shares
    rows = SIDE // parts
    planes = PAIR * depth_planes
    middle = first_kernel.shape[3] * shares
    channels = share * shares
    own_mid = first_kernel.shape[3]
    own_out = second_kernel.shape[3]
    framed = jnp.pad(features, ((0, 0), (0, 0), (REACH * SIDE, REACH * SIDE)))
    biases = jnp.zeros((8, middle), jnp.float32)
    both = jnp.stack([first_bias, second_bias])
    biases = lax.dynamic_update_slice(biases, both, (0, lax.axis_index("filt") * own_mid))
    span = (rows + 2 * REACH) * SIDE
    dma = pltpu.SemaphoreType.DMA
    return pl.pallas_call(
        functools.partial(kernel, shares, count, depth_planes),
        out_shape=jax.ShapeDtypeStruct((depth_planes, own_out, SIDE * SIDE), jnp.bfloat16),
        in_specs=[pl.BlockSpec(memory_space=pl.ANY)] * 4,
        out_specs=pl.BlockSpec(memory_space=pl.ANY),
        scratch_shapes=[
            pltpu.VMEM((4, shares, depth_planes, share, span), jnp.bfloat16),
            pltpu.VMEM((4 * depth_planes, span, 3 * channels), jnp.bfloat16),
            pltpu.VMEM((planes + 2, (rows + 2) * SIDE, 3 * middle), jnp.bfloat16),
            pltpu.VMEM((shares, 9, own_mid, 3 * channels), jnp.bfloat16),
            pltpu.VMEM((shares, 9, own_out, 3 * middle), jnp.bfloat16),
            pltpu.VMEM((shares, 8, middle), jnp.float32),
            pltpu.VMEM((planes, own_out * shares, rows * SIDE), jnp.bfloat16),
            dma((parts,)), dma((parts,)), dma((2,)), dma((2,)),
            dma((2, 2, shares // 2)), dma((2, 2, shares // 2)),
            dma((shares,)), dma((shares,)),
            dma((planes, shares)), dma((depth_planes, parts)), dma((4,)),
        ],
        compiler_params=pltpu.CompilerParams(
            collective_id=0, has_side_effects=True, vmem_limit_bytes=52 * 1024 * 1024
        ),
        cost_estimate=pl.CostEstimate(
            flops=20_000_000_000, bytes_accessed=10_000_000, transcendentals=0
        ),
    )(framed, joined(first_kernel), joined(second_kernel), biases)


def solution(mesh):
    in_specs = (
        P("depth", "filt", None),
        P(None, None, None, "filt", None),
        P("filt"),
        P(None, None, None, "filt", None),
        P("filt"),
    )
    out_specs = P("depth", "filt", None)
    return jax.shard_map(local, mesh=mesh, in_specs=in_specs, out_specs=out_specs, check_vma=False)
```

time: 118 us -> 71.3 us (0.60)
  Pallas kernels: 0 us -> 63.5 us
  blocking collectives: 39.6 us -> 0 us
  matrix products: 25.5 us -> 0 us
  waiting for transfers between devices: 16.9 us -> 0 us
  between operations: 14.3 us -> 0.07 us
  local copies, waits for them, and re-layouts: 14.5 us -> 6.71 us
  starting transfers between devices: 5.67 us -> 0 us
    pallas_call x0 -> x1, Pallas kernels: none -> 63.5 us  [local(): pl.pallas_call(functools.partial(kernel, shares, count, depth_planes), ou...]
    all_to_all x2 -> x0, blocking collectives: 33.7 us -> none  [the longest x1 16.9 us: local(): return lax.all_to_all(flat, 'filt', 1, 2, tiled=True)]
    conv_general_dilated x2 -> x0, matrix products: 25.5 us -> none  [convolve(): lax.conv_general_dilated(volume[None], kernel, (1, 1, 1), ((0, 0), (0, 0)...]
    ppermute x2 -> x0, waiting for transfers between devices: 15.5 us -> none  [the longest x1 15.5 us: depth_padded(): low = lax.ppermute(block[block.shape[0] - width:], 'depth', forward)]
    unnamed x1 -> x0, blocking collectives: 5.93 us -> none
    ppermute x2 -> x0, starting transfers between devices: 5.63 us -> none  [the longest x1 4.35 us: depth_padded(): low = lax.ppermute(block[block.shape[0] - width:], 'depth', forward)]
    reshape x0 -> x4, local copies, waits for them, and re-layouts: none -> 3.75 us  [the longest x2 2.32 us: joined(): taps = kernel_part.reshape((9, 3) + kernel_part.shape[3:])]
    conv_general_dilated x5 -> x0, local copies, waits for them, and re-layouts: 2.51 us -> none  [convolve(): lax.conv_general_dilated(volume[None], kernel, (1, 1, 1), ((0, 0), (0, 0)...]
  transfers between devices with their start and end apart: 4 -> 0, of which waited for: 1 -> 0; matrix products, arithmetic and copies ran while one was open for 18% -> 0% of each run, Pallas kernels for 0% -> 0%
where the time goes in v2:
time: 71.3 us; the launch traced here: 71 us
  Pallas kernels  63.5 us (89%)
  local copies, waits for them, and re-layouts  6.71 us (9%)
    pallas_call x1, Pallas kernels, local(): pl.pallas_call(functools.partial(kernel, shares, count, depth_planes), ou...  63.5 us
    unnamed x5, local copies, waits for them, and re-layouts  2.55 us
    reshape x2, local copies, waits for them, and re-layouts, joined(): taps = kernel_part.reshape((9, 3) + kernel_part.shape[3:])  2.32 us
    reshape x2, local copies, waits for them, and re-layouts, joined(): return jnp.transpose(taps, (0, 2, 1, 3)).reshape(9, taps.shape[2], -1)  1.43 us

profile of v2, /device:TPU:0, one launch (start us, length us, event | category | flops | bytes accessed | tf_op | source)
XLA Modules:
  0.0 71.0 jit_solution(16090943191915419341)
XLA Ops:
  0.0 0.7 pad_maximum_fusion
  0.7 0.4 dynamic_update_slice.3.b_ref
  1.1 1.9 %copy.12 = bf16[9,3,64,256]{3,1,2,0:T(4,128)(2,1)S(1)} copy(bf16[9,3,64,256]{3,2,1,0:T(8,128)(2,1)} %bitcast.12) | data formatting | bytes 1769472 | tf_op jit(solution)/shard_map/reshape | solution.py:291
  3.0 0.0 copy-start.1
  3.0 1.1 %reshape.15.k2_ref = bf16[9,64,768]{2,1,0:T(8,128)(2,1)S(1)} reshape(bf16[9,64,3,256]{3,2,1,0:T(4,128)(2,1)S(1)} %bitcast.10) | data formatting | bytes 1769472 | tf_op jit(solution)/shard_map/reshape | solution.py:292
  4.1 0.0 copy-start
  4.1 0.0 copy-done.1
  4.1 0.4 copy.13
  4.5 0.4 reshape.13.k1_ref
  4.9 0.2 copy-done
  5.2 63.5 %shard_map.55 = bf16[2,64,4096]{2,1,0:T(8,128)(2,1)} custom-call(bf16[2,32,4352]{2,1,0:T(8,128)(2,1)S(1)} %pad.4.x_ref, bf16[9,64,384]{2,1,0:T(8,128)(2,1)S(1)} %reshape.13.k1_ref, bf16[9,64,768]{2,1,0:T(8,128)(2,1)S(1)} %reshape.15.k2_ref, f32[8,256]{1,0:T(8,128)S(1)} %dynamic_update_slice.3.b_ref), custom_call_target="tpu_custom_call" | custom-call | flops 20000000000 | bytes 10000000 | tf_op jit(solution)/shard_map/pallas_call | solution.py:312
  68.7 2.3 %copy.16 = bf16[2,64,4096]{2,1,0:T(8,128)(2,1)} copy(bf16[2,64,4096]{2,1,0:T(8,128)(2,1)} %shard_map.55) | data formatting | bytes 2097152
  (2 shorter events, 0.0 us)
Async XLA Ops:
  3.0 1.1 %copy-start.1 = (bf16[3,3,3,64,128]{4,3,2,1,0:T(8,128)(2,1)S(1)}, bf16[3,3,3,64,128]{4,3,2,1,0:T(8,128)(2,1)}, u32[]{:S(2)}) copy-start(bf16[3,3,3,64,128]{4,3,2,1,0:T(8,128)(2,1)} %param.6) | copy-start | bytes 1327108
  4.1 1.0 %copy-start = (bf16[2,32,4096]{2,1,0:T(8,128)(2,1)S(1)}, bf16[2,32,4096]{2,1,0:T(8,128)(2,1)}, u32[]{:S(2)}) copy-start(bf16[2,32,4096]{2,1,0:T(8,128)(2,1)} %param.5) | copy-start | bytes 1572868

commit v3 on v2

--- a/solution.py
+++ b/solution.py
@@ -32,18 +32,25 @@
 
 
 def tap_sum(buffer, kernels, shares, plane, cells):
-    total = None
-    for tap_d in range(3):
-        for tap_h in range(3):
-            window = buffer[plane + tap_d, tap_h * SIDE : tap_h * SIDE + cells, :]
-            weights = jnp.concatenate(
-                [kernels[i, 3 * tap_d + tap_h] for i in range(shares)], axis=0
-            )
-            term = lax.dot_general(
-                window, weights, (((1,), (1,)), ((), ())), preferred_element_type=jnp.float32
-            )
-            total = term if total is None else total + term
-    return total
+    window = jnp.concatenate(
+        [
+            buffer[plane + tap_d, tap_h * SIDE : tap_h * SIDE + cells, :]
+            for tap_d in range(3)
+            for tap_h in range(3)
+        ],
+        axis=1,
+    )
+    weights = jnp.concatenate(
+        [
+            jnp.concatenate([kernels[i, tap, half] for tap in range(27)], axis=1)
+            for i in range(shares)
+            for half in range(2)
+        ],
+        axis=0,
+    )
+    return lax.dot_general(
+        window, weights, (((1,), (1,)), ((), ())), preferred_element_type=jnp.float32
+    )
 
 
 def kernel(
@@ -91,21 +98,27 @@
             device_id=home(to), device_id_type=MESH,
         )
 
-    def w_first(layer, ref, dest, m):
-        to = mate if m == 0 else (f + 2 * m) % shares
+    def w_copy(layer, stage, m, source_ref, dest_ref, to):
         return pltpu.make_async_remote_copy(
-            src_ref=ref, dst_ref=dest.at[f],
-            send_sem=w_send.at[layer, 0, m], recv_sem=w_recv.at[layer, 0, m],
-            device_id=(where, to), device_id_type=MESH,
-        )
-
-    def w_second(layer, dest, m):
+            src_ref=source_ref, dst_ref=dest_ref,
+            send_sem=w_send.at[layer, stage, m], recv_sem=w_recv.at[layer, stage, m],
+            device_id=to, device_id_type=MESH,
+        )
+
+    twin = base + 1 - side
+
+    def w_whole(layer, ref, dest):
+        return w_copy(layer, 0, 0, ref, dest.at[f], (where, mate))
+
+    def w_half(layer, ref, dest, m):
+        return w_copy(
+            layer, 0, m, ref.at[:, side], dest.at[f, :, side], (where, (f + 2 * m) % shares)
+        )
+
+    def w_pass(layer, stage, dest, m):
         source = (f - 2 * m + shares) % shares
-        return pltpu.make_async_remote_copy(
-            src_ref=dest.at[source], dst_ref=dest.at[source],
-            send_sem=w_send.at[layer, 1, m], recv_sem=w_recv.at[layer, 1, m],
-            device_id=(where, mate), device_id_type=MESH,
-        )
+        piece = dest.at[source, :, (1 - side) if stage == 3 else side]
+        return w_copy(layer, stage, m, piece, piece, (twin, f) if stage == 1 else (where, mate))
 
     def b_copy(k):
         return pltpu.make_async_remote_copy(
@@ -115,10 +128,12 @@
 
     chips = shares // 2
     x_copies = [x_copy(k) for k in range(1, parts)]
-    first1 = [w_first(0, k1_ref, k1_all, m) for m in range(chips)]
-    first2 = [w_first(1, k2_ref, k2_all, m) for m in range(chips)]
-    second1 = [w_second(0, k1_all, m) for m in range(1, chips)]
-    second2 = [w_second(1, k2_all, m) for m in range(1, chips)]
+    far = range(1, chips)
+    mates = [w_whole(0, k1_ref, k1_all), w_whole(1, k2_ref, k2_all)]
+    halves1 = [w_half(0, k1_ref, k1_all, m) for m in far]
+    halves2 = [w_half(1, k2_ref, k2_all, m) for m in far]
+    passes1 = [[w_pass(0, stage, k1_all, m) for m in far] for stage in (1, 2, 3)]
+    passes2 = [[w_pass(1, stage, k2_all, m) for m in far] for stage in (1, 2, 3)]
     b_copies = [b_copy(k) for k in range(1, shares)]
     own = [
         pltpu.make_async_copy(
@@ -129,7 +144,7 @@
         pltpu.make_async_copy(k2_ref, k2_all.at[f], own_sem.at[2]),
         pltpu.make_async_copy(b_ref, b_all.at[f], own_sem.at[3]),
     ]
-    for copy in x_copies + own + first1 + b_copies:
+    for copy in x_copies + own + halves1 + mates[:1] + b_copies:
         copy.start()
     own[0].wait()
     for copy in x_copies:
@@ -152,7 +167,7 @@
     def _():
         down_copy.start()
 
-    for copy in first2:
+    for copy in halves2 + mates[1:]:
         copy.start()
 
     @pl.when(jnp.logical_not(below))
@@ -173,35 +188,52 @@
     def _(plane):
         turn(plane)
 
-    for copy in first1:
-        copy.wait_recv()
-    for copy in second1:
-        copy.start()
-
-    @pl.when(below)
-    def _():
-        up_copy.wait_recv()
-
-    @pl.when(above)
-    def _():
-        down_copy.wait_recv()
-
-    @pl.loop(0, depth_planes)
-    def _(plane):
-        turn(plane)
-        turn(plane + 3 * depth_planes)
-
+    def relay(halves, passes):
+        for copy in halves:
+            copy.wait_recv()
+        for copy in passes[0] + passes[1]:
+            copy.start()
+
+    def finish(passes):
+        for copy in passes[0]:
+            copy.wait_recv()
+        for copy in passes[2]:
+            copy.start()
+        for copy in passes[1] + passes[2]:
+            copy.wait_recv()
+
+    relay(halves1, passes1)
     own[1].wait()
     own[3].wait()
-    for copy in second1 + b_copies:
+    for copy in b_copies + mates[:1]:
         copy.wait_recv()
+    finish(passes1)
     bias = jnp.sum(b_all[...], axis=0)
     wide = (rows + 2) * SIDE
     low_row = part * rows - 1
     low_plane = base * depth_planes - 1
 
     @pl.loop(0, planes + 2)
-    def _(plane):
+    def _(step):
+        @pl.when(step == 2)
+        def _():
+            @pl.when(below)
+            def _():
+                up_copy.wait_recv()
+
+            @pl.when(above)
+            def _():
+                down_copy.wait_recv()
+
+            @pl.loop(0, 2 * depth_planes)
+            def _(i):
+                turn((i // depth_planes) * (2 * depth_planes) + i)
+
+        @pl.when(step == 4)
+        def _():
+            relay(halves2, passes2)
+
+        plane = (step + 2) % 4 + 2 * (step // 4)
         hidden = activate(tap_sum(taps1, k1_all, shares, plane, wide), bias[0:1])
         row = low_row + lax.broadcasted_iota(jnp.int32, (wide, 1), 0) // SIDE
         deep = low_plane + plane
@@ -209,12 +241,9 @@
         spread(jnp.where(usable, hidden, 0.0), taps2, plane)
 
     own[2].wait()
-    for copy in first2:
+    for copy in mates[1:]:
         copy.wait_recv()
-    for copy in second2:
-        copy.start()
-    for copy in second2:
-        copy.wait_recv()
+    finish(passes2)
     cells = rows * SIDE
     share = results.shape[1] // shares
 
@@ -225,12 +254,17 @@
         level = plane % depth_planes
         lanes = pl.ds(pl.multiple_of(part * cells, 128), cells)
         source = results.at[plane, pl.ds(pl.multiple_of(to * share, share), share), :]
-        remote = pltpu.make_async_remote_copy(
-            src_ref=source, dst_ref=out_ref.at[level, :, lanes],
-            send_sem=o_send.at[plane, k], recv_sem=o_recv.at[level, gap],
-            device_id=home(goal), device_id_type=MESH,
-        )
-        local = pltpu.make_async_copy(source, out_ref.at[level, :, lanes], o_send.at[plane, k])
+
+        def remote():
+            return pltpu.make_async_remote_copy(
+                src_ref=source, dst_ref=out_ref.at[level, :, lanes],
+                send_sem=o_send.at[plane, k], recv_sem=o_recv.at[level, gap],
+                device_id=home(goal), device_id_type=MESH,
+            )
+
+        def local():
+            return pltpu.make_async_copy(source, out_ref.at[level, :, lanes], o_send.at[plane, k])
+
         return gap, remote, local
 
     @pl.loop(0, planes)
@@ -243,14 +277,14 @@
 
                 @pl.when(gap == 0)
                 def _():
-                    local.start()
+                    local().start()
 
                 @pl.when(gap != 0)
                 def _():
-                    remote.start()
+                    remote().start()
 
             else:
-                remote.start()
+                remote().start()
 
     for level in range(depth_planes):
         for gap in range(1, parts):
@@ -267,15 +301,15 @@
 
                 @pl.when(gap == 0)
                 def _():
-                    local.wait()
+                    local().wait()
 
                 @pl.when(gap != 0)
                 def _():
-                    remote.wait_send()
+                    remote().wait_send()
 
             else:
-                remote.wait_send()
-    for copy in x_copies + first1 + first2 + second1 + second2 + b_copies:
+                remote().wait_send()
+    for copy in x_copies + mates + halves1 + halves2 + sum(passes1 + passes2, []) + b_copies:
         copy.wait_send()
 
     @pl.when(above)
@@ -287,9 +321,8 @@
         down_copy.wait_send()
 
 
-def joined(kernel_part):
-    taps = kernel_part.reshape((9, 3) + kernel_part.shape[3:])
-    return jnp.transpose(taps, (0, 2, 1, 3)).reshape(9, taps.shape[2], -1)
+def halved(kernel_part):
+    return kernel_part.reshape(27, 2, kernel_part.shape[3] // 2, kernel_part.shape[4])
 
 
 def local(features, first_kernel, first_bias, second_kernel, second_bias):
@@ -318,12 +351,12 @@
             pltpu.VMEM((4, shares, depth_planes, share, span), jnp.bfloat16),
             pltpu.VMEM((4 * depth_planes, span, 3 * channels), jnp.bfloat16),
             pltpu.VMEM((planes + 2, (rows + 2) * SIDE, 3 * middle), jnp.bfloat16),
-            pltpu.VMEM((shares, 9, own_mid, 3 * channels), jnp.bfloat16),
-            pltpu.VMEM((shares, 9, own_out, 3 * middle), jnp.bfloat16),
+            pltpu.VMEM((shares, 27, 2, own_mid // 2, channels), jnp.bfloat16),
+            pltpu.VMEM((shares, 27, 2, own_out // 2, middle), jnp.bfloat16),
             pltpu.VMEM((shares, 8, middle), jnp.float32),
             pltpu.VMEM((planes, own_out * shares, rows * SIDE), jnp.bfloat16),
             dma((parts,)), dma((parts,)), dma((2,)), dma((2,)),
-            dma((2, 2, shares // 2)), dma((2, 2, shares // 2)),
+            dma((2, 4, shares // 2)), dma((2, 4, shares // 2)),
             dma((shares,)), dma((shares,)),
             dma((planes, shares)), dma((depth_planes, parts)), dma((4,)),
         ],
@@ -333,7 +366,7 @@
         cost_estimate=pl.CostEstimate(
             flops=20_000_000_000, bytes_accessed=10_000_000, transcendentals=0
         ),
-    )(framed, joined(first_kernel), joined(second_kernel), biases)
+    )(framed, halved(first_kernel), halved(second_kernel), biases)
 
 
 def solution(mesh):

time: 71.3 us -> 69.6 us (0.976)
  local copies, waits for them, and re-layouts: 6.71 us -> 4.75 us
    reshape x4 -> x0, local copies, waits for them, and re-layouts: 3.75 us -> none  [the longest x2 2.32 us: joined(): taps = kernel_part.reshape((9, 3) + kernel_part.shape[3:])]
    pad x1, local copies, waits for them, and re-layouts: 0.04 us -> 1.08 us  [local(): framed = jnp.pad(features, ((0, 0), (0, 0), (REACH * SIDE, REACH * SIDE)))]
    unnamed x5, local copies, waits for them, and re-layouts: 2.55 us -> 3.3 us
where the time goes in v3:
time: 69.6 us; the launch traced here: 69.4 us
  Pallas kernels  63.8 us (92%)
  local copies, waits for them, and re-layouts  4.75 us (7%)
  other arithmetic  0.76 us (1%)
    pallas_call x1, Pallas kernels, local(): pl.pallas_call(functools.partial(kernel, shares, count, depth_planes), ou...  63.8 us
    unnamed x5, local copies, waits for them, and re-layouts  3.3 us

profile of v3, /device:TPU:0, one launch (start us, length us, event | category | flops | bytes accessed | tf_op | source)
XLA Modules:
  0.0 69.4 jit_solution(10611365420411477342)
XLA Ops:
  0.0 0.0 copy-start
  0.0 0.8 %pad_maximum_fusion = f32[2,64]{1,0:T(2,128)S(1)} fusion(f32[1,64]{1,0:T(1,128)} %bitcast.6, f32[1,64]{1,0:T(1,128)} %bitcast.7), kind=kLoop, calls=%fused_computation | loop fusion | flops 128 | bytes 1024 | tf_op jit(solution)/shard_map/stack | solution.py:341
  0.8 0.4 dynamic_update_slice.3.b_ref
  1.1 1.1 %pad.4.x_ref = bf16[2,32,4352]{2,1,0:T(8,128)(2,1)S(1)} pad(bf16[2,32,4096]{2,1,0:T(8,128)(2,1)} %param.5, bf16[]{:T(256)} %constant.2.clone.1), padding=0_0x0_0x128_128 | pad | bytes 1081346 | tf_op jit(solution)/shard_map/jit(_pad)/pad | solution.py:339
  2.2 0.0 copy-done
  2.2 0.0 copy-start.1
  2.3 1.0 %copy-done.1 = bf16[3,3,3,64,128]{4,3,2,1,0:T(8,128)(2,1)S(1)} copy-done((bf16[3,3,3,64,128]{4,3,2,1,0:T(8,128)(2,1)S(1)}, bf16[3,3,3,64,128]{4,3,2,1,0:T(8,128)(2,1)}, u32[]{:S(2)}) %copy-start.1) | copy-done | bytes 442392
  3.3 63.8 %shard_map.55 = bf16[2,64,4096]{2,1,0:T(8,128)(2,1)} custom-call(bf16[2,32,4352]{2,1,0:T(8,128)(2,1)S(1)} %pad.4.x_ref, bf16[27,2,32,128]{3,2,1,0:T(8,128)(2,1)S(1)} %bitcast.5, bf16[27,2,32,256]{3,2,1,0:T(8,128)(2,1)S(1)} %bitcast.4, f32[8,256]{1,0:T(8,128)S(1)} %dynamic_update_slice.3.b_ref), custom_call_target="tpu_custom_call" | custom-call | flops 20000000000 | bytes 10000000 | tf_op jit(solution)/shard_map/pallas_call | solution.py:345
  67.1 2.3 %copy.8 = bf16[2,64,4096]{2,1,0:T(8,128)(2,1)} copy(bf16[2,64,4096]{2,1,0:T(8,128)(2,1)} %shard_map.55) | data formatting | bytes 2097152
  (1 shorter events, 0.0 us)
Async XLA Ops:
  0.0 2.2 %copy-start = (bf16[3,3,3,64,256]{4,3,2,1,0:T(8,128)(2,1)S(1)}, bf16[3,3,3,64,256]{4,3,2,1,0:T(8,128)(2,1)}, u32[]{:S(2)}) copy-start(bf16[3,3,3,64,256]{4,3,2,1,0:T(8,128)(2,1)} %param.8) | copy-start | bytes 2654212
  2.2 1.0 %copy-start.1 = (bf16[3,3,3,64,128]{4,3,2,1,0:T(8,128)(2,1)S(1)}, bf16[3,3,3,64,128]{4,3,2,1,0:T(8,128)(2,1)}, u32[]{:S(2)}) copy-start(bf16[3,3,3,64,128]{4,3,2,1,0:T(8,128)(2,1)} %param.6) | copy-start | bytes 1327108

commit v4 on v3

--- a/solution.py
+++ b/solution.py
@@ -144,7 +144,7 @@
         pltpu.make_async_copy(k2_ref, k2_all.at[f], own_sem.at[2]),
         pltpu.make_async_copy(b_ref, b_all.at[f], own_sem.at[3]),
     ]
-    for copy in x_copies + own + halves1 + mates[:1] + b_copies:
+    for copy in x_copies + own + halves1 + halves2 + mates + b_copies:
         copy.start()
     own[0].wait()
     for copy in x_copies:
@@ -166,9 +166,6 @@
     @pl.when(below)
     def _():
         down_copy.start()
-
-    for copy in halves2 + mates[1:]:
-        copy.start()
 
     @pl.when(jnp.logical_not(below))
     def _():

time: 69.6 us -> 74.8 us (1.075)
  Pallas kernels: 63.8 us -> 69.1 us
    pallas_call x1, Pallas kernels: 63.8 us -> 69.1 us  [local(): pl.pallas_call(functools.partial(kernel, shares, count, depth_planes), ou...]
where the time goes in v4:
time: 74.8 us; the launch traced here: 74.6 us
  Pallas kernels  69.1 us (92%)
  local copies, waits for them, and re-layouts  4.75 us (6%)
  other arithmetic  0.76 us (1%)
    pallas_call x1, Pallas kernels, local(): pl.pallas_call(functools.partial(kernel, shares, count, depth_planes), ou...  69.1 us
    unnamed x5, local copies, waits for them, and re-layouts  3.3 us

profile of v4, /device:TPU:0, one launch (start us, length us, event | category | flops | bytes accessed | tf_op | source)
XLA Modules:
  0.0 74.6 jit_solution(5994971623426582862)
XLA Ops:
  0.0 0.0 copy-start
  0.0 0.8 %pad_maximum_fusion = f32[2,64]{1,0:T(2,128)S(1)} fusion(f32[1,64]{1,0:T(1,128)} %bitcast.6, f32[1,64]{1,0:T(1,128)} %bitcast.7), kind=kLoop, calls=%fused_computation | loop fusion | flops 128 | bytes 1024 | tf_op jit(solution)/shard_map/stack | solution.py:338
  0.8 0.4 dynamic_update_slice.3.b_ref
  1.1 1.1 %pad.4.x_ref = bf16[2,32,4352]{2,1,0:T(8,128)(2,1)S(1)} pad(bf16[2,32,4096]{2,1,0:T(8,128)(2,1)} %param.5, bf16[]{:T(256)} %constant.2.clone.1), padding=0_0x0_0x128_128 | pad | bytes 1081346 | tf_op jit(solution)/shard_map/jit(_pad)/pad | solution.py:336
  2.2 0.0 copy-done
  2.2 0.0 copy-start.1
  2.3 1.0 %copy-done.1 = bf16[3,3,3,64,128]{4,3,2,1,0:T(8,128)(2,1)S(1)} copy-done((bf16[3,3,3,64,128]{4,3,2,1,0:T(8,128)(2,1)S(1)}, bf16[3,3,3,64,128]{4,3,2,1,0:T(8,128)(2,1)}, u32[]{:S(2)}) %copy-start.1) | copy-done | bytes 442392
  3.3 69.1 %shard_map.55 = bf16[2,64,4096]{2,1,0:T(8,128)(2,1)} custom-call(bf16[2,32,4352]{2,1,0:T(8,128)(2,1)S(1)} %pad.4.x_ref, bf16[27,2,32,128]{3,2,1,0:T(8,128)(2,1)S(1)} %bitcast.5, bf16[27,2,32,256]{3,2,1,0:T(8,128)(2,1)S(1)} %bitcast.4, f32[8,256]{1,0:T(8,128)S(1)} %dynamic_update_slice.3.b_ref), custom_call_target="tpu_custom_call" | custom-call | flops 20000000000 | bytes 10000000 | tf_op jit(solution)/shard_map/pallas_call | solution.py:342
  72.3 2.3 %copy.8 = bf16[2,64,4096]{2,1,0:T(8,128)(2,1)} copy(bf16[2,64,4096]{2,1,0:T(8,128)(2,1)} %shard_map.55) | data formatting | bytes 2097152
  (1 shorter events, 0.0 us)
Async XLA Ops:
  0.0 2.2 %copy-start = (bf16[3,3,3,64,256]{4,3,2,1,0:T(8,128)(2,1)S(1)}, bf16[3,3,3,64,256]{4,3,2,1,0:T(8,128)(2,1)}, u32[]{:S(2)}) copy-start(bf16[3,3,3,64,256]{4,3,2,1,0:T(8,128)(2,1)} %param.8) | copy-start | bytes 2654212
  2.2 1.0 %copy-start.1 = (bf16[3,3,3,64,128]{4,3,2,1,0:T(8,128)(2,1)S(1)}, bf16[3,3,3,64,128]{4,3,2,1,0:T(8,128)(2,1)}, u32[]{:S(2)}) copy-start(bf16[3,3,3,64,128]{4,3,2,1,0:T(8,128)(2,1)} %param.6) | copy-start | bytes 1327108
